TPU v7x, 128 devices: a whole 4x4x4 slice. The times are simulated.
128 devices in a mesh: dp: 8 (over y_hi, x), tensor: 16 (over z, y_lo, core).
Axes of the slice: x: 4, y: 4 (y_hi: 2, y_lo: 2; y = y_hi * 2 + y_lo), z: 4, core: 2. Of those that a mesh axis runs over, the one named last changes fastest.
Arguments:
- queries: bfloat16 [16384, 8192], P(('dp', 'tensor')), may hold values from -128 to 128
- keys: bfloat16 [16384, 512], P(('dp', 'tensor')), may hold values from -8 to 8
- values: bfloat16 [16384, 512], P(('dp', 'tensor')), may hold values from -6 to 6
- saved_out: bfloat16 [16384, 8192], P(('dp', 'tensor')), may hold values from -6 to 6
- grad_out: bfloat16 [16384, 8192], P(('dp', 'tensor')), may hold values from -24 to 24
- normed_input: bfloat16 [16384, 8192], P(('dp', 'tensor')), may hold values from -24 to 24
- subtree_end: int32 [16384], P('dp'), may hold values from 0 to 2047, as said below
Outputs:
- grad_queries: bfloat16 [16384, 8192], P(('dp', 'tensor'))
- grad_keys: bfloat16 [16384, 512], P(('dp', 'tensor'))
- grad_values: bfloat16 [16384, 512], P(('dp', 'tensor'))
- grad_wk: float32 [8192, 512], P(('dp', 'tensor'))
- grad_wv: float32 [8192, 512], P(('dp', 'tensor'))
Inputs may be any that keep to these rules, and one draw needn't show every extreme that they name: Each group of 2048 tokens is a forest in pre-order: subtree_end[j] is at least j, at most the group's last position, and subtrees nest.
All inputs are finite; a program needn't handle non-finite values.
Results may differ from a plain program's by a relative error of at most 0.005.
Values may be sent and summed in bfloat16 or wider, within the bound.
A program may use at most 448 MiB of HBM per device.

v0:
```python
import math

import jax
import jax.numpy as jnp
from jax import lax
from jax.sharding import PartitionSpec as P

D = 8192
HQ = 64
KVH = 4
HD = 128


def over_blocks(carry, arrays, start, advance):
    count = arrays[0].shape[0]
    block = math.gcd(count, 512)

    def looped(step_index, state):
        offset = step_index * block
        pieces = tuple((lax.dynamic_slice_in_dim(whole, offset, block, 0) for whole in arrays))
        return advance(state, pieces, start + offset)

    return lax.fori_loop(0, count // block, looped, carry)


def gather_rows(grad_keys, grad_values):
    return (
        lax.all_gather(grad_keys, "tensor", axis=0, tiled=True),
        lax.all_gather(grad_values, "tensor", axis=0, tiled=True),
    )


def shards(queries, keys, values, saved_out, grad_out, normed_input, subtree_end):
    row_count = queries.shape[0]
    tensor_count = lax.axis_size("tensor")
    group_tokens = row_count * tensor_count
    head_group = HQ // KVH
    softmax_scale = HD ** (-0.5)
    query_heads = queries.reshape(row_count, KVH, head_group, HD)
    grad_heads = grad_out.reshape(row_count, KVH, head_group, HD)
    out_heads = saved_out.reshape(row_count, KVH, head_group, HD)
    out_dot = jnp.einsum(
        "rgqd,rgqd->gqr", grad_heads, out_heads, preferred_element_type=jnp.float32
    )
    query_place = lax.axis_index("tensor") * row_count + jnp.arange(row_count, dtype=jnp.int32)

    def allowed_for(start, count):
        key_place = start + jnp.arange(count, dtype=jnp.int32)
        key_end = lax.dynamic_slice_in_dim(subtree_end, start, count, 0)
        return (key_place[None, :] <= query_place[:, None]) & (
            query_place[:, None] <= key_end[None, :]
        )

    def scores_for(key_block):
        key_heads = key_block.reshape(-1, KVH, HD)
        return (
            jnp.einsum("rgqd,bgd->gqrb", query_heads, key_heads, preferred_element_type=jnp.float32)
            * softmax_scale
        )

    def total_step(carry, pieces, start):
        key_block = pieces[0]
        allowed = allowed_for(start, key_block.shape[0])

        def total_active(state):
            highest, totals = state
            scores = scores_for(key_block)
            raised = jnp.maximum(highest, jnp.max(jnp.where(allowed, scores, -1e30), axis=-1))
            totals = totals * jnp.exp(highest - raised) + jnp.sum(
                jnp.where(allowed, jnp.exp(scores - raised[..., None]), 0.0), axis=-1
            )
            return (raised, totals)

        return lax.cond(jnp.any(allowed), total_active, lambda state: state, carry)

    start_totals = (
        jnp.full((KVH, head_group, row_count), -1e30, jnp.float32),
        jnp.zeros((KVH, head_group, row_count), jnp.float32),
    )

    def gradient_step_with(log_total):

        def gradient_step(carry, pieces, start):
            key_block, value_block = pieces
            allowed = allowed_for(start, key_block.shape[0])

            def gradient_active(state):
                query_acc, key_all, value_all = state
                key_heads = key_block.reshape(-1, KVH, HD)
                value_heads = value_block.reshape(-1, KVH, HD)
                scores = scores_for(key_block)
                prob = jnp.where(allowed, jnp.exp(scores - log_total[..., None]), 0.0)
                prob_b = prob.astype(jnp.bfloat16)
                dprob = jnp.einsum(
                    "rgqd,bgd->gqrb", grad_heads, value_heads, preferred_element_type=jnp.float32
                )
                dscore_b = (prob * (dprob - out_dot[..., None])).astype(jnp.bfloat16)
                query_acc = query_acc + jnp.einsum(
                    "gqrb,bgd->rgqd", dscore_b, key_heads, preferred_element_type=jnp.float32
                )
                key_part = (
                    jnp.einsum(
                        "gqrb,rgqd->bgd", dscore_b, query_heads, preferred_element_type=jnp.float32
                    )
                    * softmax_scale
                )
                value_part = jnp.einsum(
                    "gqrb,rgqd->bgd", prob_b, grad_heads, preferred_element_type=jnp.float32
                )
                key_all = lax.dynamic_update_slice_in_dim(key_all, key_part, start, 0)
                value_all = lax.dynamic_update_slice_in_dim(value_all, value_part, start, 0)
                return (query_acc, key_all, value_all)

            return lax.cond(jnp.any(allowed), gradient_active, lambda state: state, carry)

        return gradient_step

    empty_keys = jnp.zeros((group_tokens, KVH, HD), jnp.float32)
    start_grads = (jnp.zeros((row_count, KVH, head_group, HD), jnp.float32), empty_keys, empty_keys)
    key_group, value_group = (
        lax.all_gather(keys, "tensor", axis=0, tiled=True),
        lax.all_gather(values, "tensor", axis=0, tiled=True),
    )
    highest, totals = over_blocks(start_totals, (key_group,), 0, total_step)
    log_total = highest + jnp.log(totals)
    query_acc, key_all, value_all = over_blocks(
        start_grads, (key_group, value_group), 0, gradient_step_with(log_total)
    )
    grad_queries = (query_acc * softmax_scale).astype(jnp.bfloat16).reshape(row_count, HQ * HD)
    key_terms = key_all.reshape(group_tokens, KVH * HD)
    value_terms = value_all.reshape(group_tokens, KVH * HD)
    key_local, value_local = (
        lax.psum_scatter(key_terms, "tensor", scatter_dimension=0, tiled=True),
        lax.psum_scatter(value_terms, "tensor", scatter_dimension=0, tiled=True),
    )
    grad_keys = key_local.astype(jnp.bfloat16)
    grad_values = value_local.astype(jnp.bfloat16)
    key_group_grad, value_group_grad = gather_rows(grad_keys, grad_values)
    group_count = lax.axis_size("dp")
    feature_width = D // (group_count * tensor_count)
    split_input = normed_input.reshape(row_count, group_count, tensor_count, feature_width)
    columns = lax.all_to_all(split_input, "tensor", split_axis=2, concat_axis=0, tiled=True)
    columns = columns.reshape(group_tokens, group_count * feature_width)
    contract = (((0,), (0,)), ((), ()))
    key_weight = lax.dot_general(
        columns, key_group_grad, contract, preferred_element_type=jnp.float32
    )
    value_weight = lax.dot_general(
        columns, value_group_grad, contract, preferred_element_type=jnp.float32
    )
    key_weight = key_weight.reshape(group_count, feature_width, KVH * HD)
    value_weight = value_weight.reshape(group_count, feature_width, KVH * HD)
    summed_keys, summed_values = (
        lax.psum_scatter(key_weight, "dp", scatter_dimension=0, tiled=True),
        lax.psum_scatter(value_weight, "dp", scatter_dimension=0, tiled=True),
    )
    grad_wk = summed_keys.reshape(feature_width, KVH * HD)
    grad_wv = summed_values.reshape(feature_width, KVH * HD)
    return (grad_queries, grad_keys, grad_values, grad_wk, grad_wv)


def solution(mesh):
    in_specs = (
        P(("dp", "tensor"), None),
        P(("dp", "tensor"), None),
        P(("dp", "tensor"), None),
        P(("dp", "tensor"), None),
        P(("dp", "tensor"), None),
        P(("dp", "tensor"), None),
        P("dp"),
    )
    out_specs = (
        P(("dp", "tensor"), None),
        P(("dp", "tensor"), None),
        P(("dp", "tensor"), None),
        P(("dp", "tensor"), None),
        P(("dp", "tensor"), None),
    )
    return jax.shard_map(shards, mesh=mesh, in_specs=in_specs, out_specs=out_specs, check_vma=False)
```

profile of v0, /device:TPU:0, one launch (start us, length us, event | category | flops | bytes accessed | tf_op | source)
XLA Modules:
  0.0 686.6 jit_solution(6430755187208664224)
XLA Ops:
  7.2 1.7 copy.38
  8.9 1.7 copy.41
  10.7 3.2 copy.42
  13.9 2.6 copy.44
  16.6 4.1 copy.39
  20.6 3.0 copy.43
  23.7 3.5 copy.76
  27.2 4.9 copy.63
  32.1 4.2 multiply_reduce_fusion
  36.4 13.7 %all-gather.5.cloned.1.call-done = bf16[2048,512]{0,1:T(8,128)(2,1)} async-done(((bf16[128,512]{0,1:T(8,128)(2,1)}), bf16[2048,512]{0,1:T(8,128)(2,1)}) %all-gather.5.cloned.1.call-update) | async-done | bytes 2097168 | tf_op jit(solution)/shard_map/all_gather | solution.py:121
  50.1 24.7 %while.34 = (s32[]{:T(128)}, f32[4,16,128]{2,1,0:T(8,128)S(1)}, f32[4,16,128]{2,1,0:T(8,128)S(1)}, s32[2048]{0:T(1024)S(1)}, bf16[2048,512]{0,1:T(8,128)(2,1)}, ...) while((s32[]{:T(128)}, f32[4,16,128]{2,1,0:T(8,128)S(1)}, ...), condition=%wide.region_6.7_spmd.clone, body=%wide.region_0.6_spmd.clone.sunk | while | flops 1103381120 | bytes 37858568 | solution.py:23
  50.2 0.9 compare_and_fusion.4
  51.7 18.0 %conditional.6 = ((f32[4,16,128]{2,1,0:T(8,128)S(1)}, f32[4,16,128]{2,1,0:T(8,128)S(1)})) conditional(s32[]{:T(128)} %convert_element_type.48, (f32[4,16,128]{2,1,0:T(8,128)S(1)}, f32[4,16,128]{2,1,0:T(8,128)S(1)}) %tuple.99, (pred[128,512]{0,1:T(8,128)(4,1)S(1)}, bf16[2048,512]{0,1:T(8,128)(2,1)}, s32[]{:T(128)}, ...), branch_computations={%region_2.0_spmd, %region_3.5_spmd} | conditional | flops 1103118336 | bytes 37781532 | solution.py:74
  51.7 1.1 constant_dynamic-slice_fusion
  52.8 7.2 %fusion.4 = (f32[4,16,128]{2,1,0:T(8,128)S(1)}, f32[4,512,128,16]{2,1,3,0:T(8,128)}) fusion(pred[128,512]{0,1:T(8,128)(4,1)S(1)} %get-tuple-element.428, bf16[512,4,128,1]{0,2,3,1:T(8,128)(2,1)S(1)} %bitcast.131, bf16[128,4,16,128]{3,0,2,1:T(8,128)(2,1)S(1)} %get-tuple-element.431), kind=kOutput, calls=%fused_computation.4 | convolution fusion | flops 1086316544 | bytes 19496960 | tf_op jit(solution)/shard_map/while/body/eval_jaxpr/cond/branch_1_fun/rgqd,bgd->gqrb/dot_general | solution.py:57
  60.0 9.7 %fusion.7 = f32[4,16,128]{2,1,0:T(8,128)S(1)} fusion(f32[4,512,128,16]{2,1,3,0:T(8,128)} %get-tuple-element.612, f32[4,16,128]{2,1,0:T(8,128)S(1)} %max.3, pred[128,512]{0,1:T(8,128)(4,1)S(1)} %get-tuple-element.428), kind=kLoop, calls=%fused_computation.7 | loop fusion | flops 16769024 | bytes 16908288 | tf_op jit(solution)/shard_map/while/body/eval_jaxpr/cond/branch_1_fun/reduce_sum | solution.py:69
  69.9 0.9 compare_and_fusion.4
  73.2 0.9 compare_and_fusion.4
  74.8 15.1 %all-gather.7.cloned.1.call-done = bf16[2048,512]{0,1:T(8,128)(2,1)} async-done(((bf16[128,512]{0,1:T(8,128)(2,1)}), bf16[2048,512]{0,1:T(8,128)(2,1)}) %all-gather.7.cloned.1.call-update) | async-done | bytes 2097168 | tf_op jit(solution)/shard_map/all_gather | solution.py:122
  89.9 2.2 broadcast_in_dim.61.clone
  92.1 2.2 broadcast_in_dim.61
  94.3 2.5 broadcast_in_dim.60
  96.8 45.1 %while.35 = (s32[]{:T(128)}, f32[128,4,16,128]{3,0,2,1:T(8,128)}, f32[2048,4,128]{2,0,1:T(8,128)}, f32[2048,4,128]{2,0,1:T(8,128)}, s32[2048]{0:T(1024)S(1)}, /*...) while((s32[]{:T(128)}, f32[128,4,16,128]{3,0,2,1:T(8,128)}, ...), condition=%wide.region_11.12_spmd.clone, body=%wide.region_7.11_spmd.clone.sunk | while | flops 5412225536 | bytes 106737080 | solution.py:23
  98.4 38.5 %conditional.7 = ((f32[128,4,16,128]{3,0,2,1:T(8,128)}, f32[2048,4,128]{2,0,1:T(8,128)}, f32[2048,4,128]{2,0,1:T(8,128)})) conditional(s32[]{:T(128)} %convert_element_type.49, (f32[128,4,16,128]{3,0,2,1:T(8,128)}, f32[2048,4,128]{2,0,1:T(8,128)}, f32[2048,4,128]{2,0,1:T(8,128)}) %tuple.103, (pred[128,512]{0,1:T(8,128)(4,1)S(1)}, ...), branch_computations={%region_9.9_spmd, %region_10.10_spmd} | conditional | flops 5411962880 | bytes 106659952 | solution.py:114
  98.4 1.3 constant_dynamic-slice_fusion.1
  99.7 8.1 %fusion.35 = f32[4,512,128,16]{2,1,3,0:T(8,128)} fusion(bf16[512,4,128,1]{0,2,3,1:T(8,128)(2,1)S(1)} %bitcast.129, bf16[128,4,16,128]{3,0,2,1:T(8,128)(2,1)S(1)} %get-tuple-element.447), kind=kOutput, calls=%fused_computation.50 | convolution fusion | flops 1073741824 | bytes 19398656 | tf_op jit(solution)/shard_map/while/body/eval_jaxpr/cond/branch_1_fun/rgqd,bgd->gqrb/dot_general | solution.py:57
  107.8 9.4 %fusion.19 = f32[2048,4,128]{2,0,1:T(8,128)} fusion(f32[2048,4,128]{2,0,1:T(8,128)} %get-tuple-element.454, s32[]{:T(128)S(6)} %select_n.35, bf16[128,4,16,128]{3,0,2,1:T(8,128)(2,1)S(1)} %copy-done.1, f32[4,512,128,16]{2,1,3,0:T(8,128)} %fusion.35, f32[4,16,128]{2,1,0:T(8,128)S(1)} %get-tuple-element.448, pred[128,512]{0,1:T(8,128)(4,1)S(1)} %get-tuple-element.444), kind=kOutput, calls=%fused_computation.21 | convolution fusion | flops 1090519040 | bytes 20021252 | tf_op jit(solution)/shard_map/while/body/eval_jaxpr/cond/branch_1_fun/gqrb,rgqd->bgd/dot_general | solution.py:107
  117.2 9.4 %fusion.9 = bf16[4,16,128,512]{2,3,1,0:T(8,128)(2,1)S(1)} fusion(f32[4,512,128,16]{2,1,3,0:T(8,128)} %fusion.35, bf16[512,4,128,1]{0,2,3,1:T(8,128)(2,1)S(1)} %bitcast.134, bf16[128,4,16,128]{3,0,2,1:T(8,128)(2,1)} %get-tuple-element.450, f32[4,16,128]{2,1,0:T(8,128)S(1)} %get-tuple-element.451, f32[4,16,128]{2,1,0:T(8,128)S(1)} %get-tuple-element.448, ...), kind=kOutput, calls=%fused_computation.12 | convolution fusion | flops 1098907648 | bytes 27918336 | tf_op jit(solution)/shard_map/while/body/eval_jaxpr/cond/branch_1_fun/rgqd,bgd->gqrb/dot_general | solution.py:94
  126.6 3.3 fusion.24
  129.9 6.9 %bitcast_add_fusion = f32[128,4,16,128]{3,0,2,1:T(8,128)} fusion(f32[128,4,16,128]{3,0,2,1:T(8,128)} %get-tuple-element.443, bf16[4,16,128,512]{2,3,1,0:T(8,128)(2,1)S(1)} %fusion.9, bf16[512,4,128,1]{0,2,3,1:T(8,128)(2,1)S(1)} %bitcast.130), kind=kOutput, calls=%fused_computation.19 | convolution fusion | flops 1074790400 | bytes 17301504 | tf_op jit(solution)/shard_map/while/body/eval_jaxpr/cond/branch_1_fun/gqrb,bgd->rgqd/dot_general | solution.py:98
  141.9 4.7 copy_bitcast_fusion
  146.8 4.7 copy_bitcast_fusion.1
  151.6 219.4 %reduce-scatter.7.cloned.1.call-done = f32[128,512]{1,0:T(8,128)} async-done(((f32[2048,512]{1,0:T(8,128)}), f32[128,512]{1,0:T(8,128)}) %reduce-scatter.7.cloned.1.call-update) | async-done | bytes 262160 | tf_op jit(solution)/shard_map/reduce_scatter | solution.py:134
  371.0 1.6 convert_element_type.35
  372.7 69.5 %reduce-scatter.5.cloned.1.call-done = f32[128,512]{1,0:T(8,128)} async-done(((f32[2048,512]{1,0:T(8,128)}), f32[128,512]{1,0:T(8,128)}) %reduce-scatter.5.cloned.1.call-update) | async-done | bytes 262160 | tf_op jit(solution)/shard_map/reduce_scatter | solution.py:133
  442.2 1.6 convert_element_type.34
  443.9 3.2 copy.48
  447.3 38.1 %all_to_all.15 = bf16[128,8,16,64]{0,3,1,2:T(8,128)(2,1)S(1)} all-to-all(bf16[128,8,16,64]{0,3,1,2:T(8,128)(2,1)S(1)} %copy.49), channel_id=1, replica_groups=mesh['dp'=8,'tensor'=16] {'tensor'}, dimensions={2} | all-to-all | bytes 4194304 | tf_op jit(solution)/shard_map/all_to_all | solution.py:142
  485.4 1.4 copy.50
  486.8 5.1 all-gather.11.cloned.1.call-done
  491.9 3.8 fusion.31
  495.8 32.3 %all-gather.9.cloned.1.call-done = bf16[2048,512]{1,0:T(8,128)(2,1)} async-done(((bf16[128,512]{1,0:T(8,128)(2,1)}), bf16[2048,512]{1,0:T(8,128)(2,1)}) %all-gather.9.cloned.1.call-update) | async-done | bytes 2097168 | tf_op jit(solution)/shard_map/all_gather | solution.py:28
  528.1 3.8 fusion.29
  532.0 2.8 multiply_convert_fusion
  534.8 1.4 copy.45
  536.1 3.1 copy.90
  539.2 64.8 %reduce-scatter.11.cloned.1.call-done = f32[1,64,512]{2,1,0:T(8,128)} async-done(((f32[8,64,512]{2,1,0:T(8,128)}), f32[1,64,512]{2,1,0:T(8,128)}) %reduce-scatter.11.cloned.1.call-update) | async-done | bytes 131088 | tf_op jit(solution)/shard_map/reduce_scatter | solution.py:155
  604.1 75.7 %reduce-scatter.9.cloned.1.call-done = f32[1,64,512]{2,1,0:T(8,128)} async-done(((f32[8,64,512]{2,1,0:T(8,128)}), f32[1,64,512]{2,1,0:T(8,128)}) %reduce-scatter.9.cloned.1.call-update) | async-done | bytes 131088 | tf_op jit(solution)/shard_map/reduce_scatter | solution.py:154
  (65 shorter events, 5.8 us)
Async XLA Ops:
  7.2 42.9 %all-gather.5.cloned.1.call-start = ((), (), s32[]{:S(2)}) async-start(), calls=%async_computation.5 | async-start | bytes 2228224 | tf_op jit(solution)/shard_map/all_gather | solution.py:121
  8.9 81.0 %all-gather.7.cloned.1.call-start = ((), (), s32[]{:S(2)}) async-start(), calls=%async_computation.6 | async-start | bytes 2228224 | tf_op jit(solution)/shard_map/all_gather | solution.py:122
  10.6 360.3 %reduce-scatter.7.cloned.1.call-start = ((), (), s32[]{:S(2)}) async-start(), calls=%async_computation.8 | async-start | bytes 4456448 | tf_op jit(solution)/shard_map/reduce_scatter | solution.py:134
  13.9 6.7 copy-start
  32.1 17.9 %copy-start.2 = (s32[2048]{0:T(1024)S(1)}, s32[2048]{0:T(1024)}, u32[]{:S(2)}) copy-start(s32[2048]{0:T(1024)} %param.21) | copy-start | bytes 24580
  99.7 8.1 %copy-start.1 = (bf16[128,4,16,128]{3,0,2,1:T(8,128)(2,1)S(1)}, bf16[128,4,16,128]{3,0,2,1:T(8,128)(2,1)}, u32[]{:S(2)}) copy-start(bf16[128,4,16,128]{3,0,2,1:T(8,128)(2,1)} %get-tuple-element.450) | copy-start | bytes 6291460 | tf_op jit(solution)/shard_map/while/body/eval_jaxpr/cond
  146.7 295.5 %reduce-scatter.5.cloned.1.call-start = ((), (), s32[]{:S(2)}) async-start(), calls=%async_computation.7 | async-start | bytes 4456448 | tf_op jit(solution)/shard_map/reduce_scatter | solution.py:133
  151.5 340.4 %all-gather.11.cloned.1.call-start = ((), (), s32[]{:S(2)}) async-start(), calls=%async_computation.11 | async-start | bytes 2228224 | tf_op jit(solution)/shard_map/all_gather | solution.py:29
  372.6 155.5 %all-gather.9.cloned.1.call-start = ((), (), s32[]{:S(2)}) async-start(), calls=%async_computation.9 | async-start | bytes 2228224 | tf_op jit(solution)/shard_map/all_gather | solution.py:28
  443.8 160.3 %reduce-scatter.11.cloned.1.call-start = ((), (), s32[]{:S(2)}) async-start(), calls=%async_computation.12 | async-start | bytes 1179648 | tf_op jit(solution)/shard_map/reduce_scatter | solution.py:155
  495.7 184.1 %reduce-scatter.9.cloned.1.call-start = ((), (), s32[]{:S(2)}) async-start(), calls=%async_computation.10 | async-start | bytes 1179648 | tf_op jit(solution)/shard_map/reduce_scatter | solution.py:154
Sparse Core Ops, SparseCore 0:
  10.2 39.8 all-gather.4
  52.3 37.5 all-gather.6
  146.8 224.0 reduce-scatter.6
  373.2 68.8 reduce-scatter.4
  444.3 47.5 all-gather.10
  494.0 34.0 all-gather.8
  532.3 71.7 reduce-scatter.10
  608.7 70.9 reduce-scatter.8
where the time goes:
time: 688 us; the launch traced here: 687 us
  waiting for transfers between devices  496 us (72%)
  local copies, waits for them, and re-layouts  53.5 us (8%)
  matrix products  52 us (8%)
  blocking collectives  38.1 us (6%)
  other arithmetic  27 us (4%)
  between operations  14.2 us (2%)
    reduce_scatter x1, waiting for transfers between devices, shards(): lax.psum_scatter(value_terms, 'tensor', scatter_dimension=0, tiled=True)  219 us
    reduce_scatter x1, waiting for transfers between devices, shards(): lax.psum_scatter(key_weight, 'dp', scatter_dimension=0, tiled=True)  75.7 us
    reduce_scatter x1, waiting for transfers between devices, shards(): lax.psum_scatter(key_terms, 'tensor', scatter_dimension=0, tiled=True)  69.5 us
    reduce_scatter x1, waiting for transfers between devices, shards(): lax.psum_scatter(value_weight, 'dp', scatter_dimension=0, tiled=True)  64.8 us
    all_to_all x1, blocking collectives, shards(): lax.all_to_all(split_input, 'tensor', split_axis=2, concat_axis=0, tiled=...  38.1 us
    all_gather x1, waiting for transfers between devices, gather_rows(): lax.all_gather(grad_keys, 'tensor', axis=0, tiled=True)  32.3 us
    unnamed x14, local copies, waits for them, and re-layouts  31.1 us
    dot_general x2, matrix products, scores_for(): jnp.einsum('rgqd,bgd->gqrb', query_heads, key_heads, preferred_element_ty...  15.3 us
  transfers between devices with their start and end apart: 8, of which 8 were waited for; matrix products, arithmetic and copies ran while one was open for 11% of the time, Pallas kernels for 0%

commit v1 on v0

v1 whole, which is shorter than its diff:
```python
import functools
import math

import jax
import jax.numpy as jnp
from jax import lax
from jax.experimental import pallas as pl
from jax.experimental.pallas import tpu as pltpu
from jax.sharding import PartitionSpec as P

D = 8192
HQ = 64
KVH = 4
HD = 128
SEQ = 2048
ROWS = 128
BLOCKS = SEQ // ROWS
HG = HQ // KVH
HB = 4
WIDTHS = (128, 256, 384, 640, SEQ - ROWS)
SCALE = HD ** (-0.5)
NT = (((1,), (1,)), ((), ()))
TN = (((0,), (0,)), ((), ()))
f32 = jnp.float32
bf16 = jnp.bfloat16


def attention_kernel(
    place_ref, end_ref, q_ref, do_ref, o_ref, k_ref, v_ref,
    dq_ref, dk_ref, dv_ref, rank, pick, bias, kc, vc,
):
    t = place_ref[0]
    g = pl.program_id(0)
    first = t * ROWS
    lane = lax.broadcasted_iota(jnp.int32, (ROWS, ROWS), 1)
    sub = lax.broadcasted_iota(jnp.int32, (ROWS, ROWS), 0)

    pos = (
        lax.broadcasted_iota(jnp.int32, (BLOCKS, ROWS), 0) * ROWS
        + lax.broadcasted_iota(jnp.int32, (BLOCKS, ROWS), 1)
    )
    far = (pos < first) & (end_ref[...] >= first)
    n_far = jnp.sum(far.astype(jnp.int32))

    @pl.when(g == 0)
    def _prepare():
        flags = far.astype(f32).astype(bf16)
        upto = (sub <= lane).astype(f32).astype(bf16)
        within = jnp.dot(flags, upto, preferred_element_type=f32)
        totals = jnp.dot(flags, jnp.ones((ROWS, ROWS), bf16), preferred_element_type=f32)
        earlier = (
            lax.broadcasted_iota(jnp.int32, (BLOCKS, BLOCKS), 1)
            < lax.broadcasted_iota(jnp.int32, (BLOCKS, BLOCKS), 0)
        )
        before = jnp.dot(
            earlier.astype(f32).astype(bf16), totals.astype(bf16), preferred_element_type=f32
        )
        rank[...] = jnp.where(far, (within + before).astype(jnp.int32) - 1, -1)
        own_end = end_ref[pl.ds(t, 1), :]
        end_col = jnp.sum(jnp.where(sub == lane, own_end, 0), axis=1, keepdims=True)
        ok = (sub <= lane) & (lane + first <= end_col)
        bias[0:ROWS, :] = jnp.where(ok, 0.0, -1e30)
        kc[0:ROWS, :] = k_ref[pl.ds(pl.multiple_of(first, ROWS), ROWS), :]
        vc[0:ROWS, :] = v_ref[pl.ds(pl.multiple_of(first, ROWS), ROWS), :]

    def run(width):
        total = width + ROWS

        @pl.when(g == 0)
        def _compact():
            def one(b, carry):
                at = pl.multiple_of(b * ROWS, ROWS)
                end_sum = jnp.zeros((ROWS, ROWS), jnp.int32)
                for r in range(BLOCKS):
                    hit = rank[r : r + 1, :] == sub + at
                    end_sum = end_sum + jnp.where(hit, end_ref[r : r + 1, :] + 1, 0)
                    pick[pl.ds(at, ROWS), r * ROWS : (r + 1) * ROWS] = hit.astype(f32).astype(bf16)
                end_col = jnp.sum(end_sum, axis=1, keepdims=True) - 1
                bias[pl.ds(at + ROWS, ROWS), :] = jnp.where(lane + first <= end_col, 0.0, -1e30)
                chosen = pick[pl.ds(at, ROWS), :]
                kc[pl.ds(at + ROWS, ROWS), :] = jnp.dot(
                    chosen, k_ref[...], preferred_element_type=f32
                ).astype(bf16)
                vc[pl.ds(at + ROWS, ROWS), :] = jnp.dot(
                    chosen, v_ref[...], preferred_element_type=f32
                ).astype(bf16)
                return carry

            lax.fori_loop(0, width // ROWS, one, 0)

        gcol = pl.multiple_of(g * HD, HD)
        kg = kc[0:total, pl.ds(gcol, HD)]
        vg = vc[0:total, pl.ds(gcol, HD)]

        def heads(i, acc):
            dk_acc, dv_acc = acc
            cols = [pl.ds(pl.multiple_of((i * HB + b) * HD, HD), HD) for b in range(HB)]
            q4 = jnp.concatenate([q_ref[:, c] for c in cols], axis=0)
            do4 = jnp.concatenate([do_ref[:, c] for c in cols], axis=0)
            o4 = jnp.concatenate([o_ref[:, c] for c in cols], axis=0)
            prod = do4.astype(f32) * o4.astype(f32)
            high = prod.astype(bf16)
            low = (prod - high.astype(f32)).astype(bf16)
            ones = jnp.ones((16, HD), bf16)
            dots = (
                lax.dot_general(ones, high, NT, preferred_element_type=f32)
                + lax.dot_general(ones, low, NT, preferred_element_type=f32)
            )[0:1, :]
            b1 = bias[0:total, :]
            b4 = jnp.concatenate([b1] * HB, axis=1)
            s = lax.dot_general(kg, q4, NT, preferred_element_type=f32) * SCALE + b4
            top = jnp.max(s, axis=0, keepdims=True)
            p = jnp.exp(s - top)
            p = p * (1.0 / jnp.sum(p, axis=0, keepdims=True))
            dp = lax.dot_general(vg, do4, NT, preferred_element_type=f32)
            ds = (p * (dp - dots)).astype(bf16)
            dq = lax.dot_general(ds, kg, TN, preferred_element_type=f32) * SCALE
            for b in range(HB):
                dq_ref[:, cols[b]] = dq[b * ROWS : (b + 1) * ROWS, :].astype(bf16)
            dk_acc = dk_acc + jnp.dot(ds, q4, preferred_element_type=f32)
            dv_acc = dv_acc + jnp.dot(p.astype(bf16), do4, preferred_element_type=f32)
            return dk_acc, dv_acc

        zero = jnp.zeros((total, HD), f32)
        dk_acc, dv_acc = lax.fori_loop(0, HG // HB, heads, (zero, zero))
        dk = (dk_acc * SCALE).astype(bf16)
        dv = dv_acc.astype(bf16)
        chosen = pick[0:width, :]
        dk_ref[...] = lax.dot_general(chosen, dk[ROWS:], TN, preferred_element_type=f32).astype(bf16)
        dv_ref[...] = lax.dot_general(chosen, dv[ROWS:], TN, preferred_element_type=f32).astype(bf16)
        dk_ref[pl.ds(pl.multiple_of(first, ROWS), ROWS), :] = dk[:ROWS]
        dv_ref[pl.ds(pl.multiple_of(first, ROWS), ROWS), :] = dv[:ROWS]

    lower = -1
    for width in WIDTHS:
        pl.when((n_far > lower) & (n_far <= width))(functools.partial(run, width))
        lower = width


def attention(queries, grad_out, saved_out, key_group, value_group, subtree_end):
    place = lax.axis_index("tensor").astype(jnp.int32).reshape(1)
    wide = pl.BlockSpec((ROWS, HG * HD), lambda g, place: (0, g))
    whole = pl.BlockSpec((SEQ, KVH * HD), lambda g, place: (0, 0))
    part = pl.BlockSpec((SEQ, HD), lambda g, place: (0, g))
    far_most = SEQ - ROWS
    return pl.pallas_call(
        attention_kernel,
        grid_spec=pltpu.PrefetchScalarGridSpec(
            num_scalar_prefetch=1,
            grid=(KVH,),
            in_specs=[
                pl.BlockSpec((BLOCKS, ROWS), lambda g, place: (0, 0)),
                wide, wide, wide, whole, whole,
            ],
            out_specs=[wide, part, part],
            scratch_shapes=[
                pltpu.VMEM((BLOCKS, ROWS), jnp.int32),
                pltpu.VMEM((far_most, SEQ), bf16),
                pltpu.VMEM((SEQ, ROWS), f32),
                pltpu.VMEM((SEQ, KVH * HD), bf16),
                pltpu.VMEM((SEQ, KVH * HD), bf16),
            ],
        ),
        out_shape=[
            jax.ShapeDtypeStruct((ROWS, HQ * HD), bf16),
            jax.ShapeDtypeStruct((SEQ, KVH * HD), bf16),
            jax.ShapeDtypeStruct((SEQ, KVH * HD), bf16),
        ],
        compiler_params=pltpu.CompilerParams(vmem_limit_bytes=56 * 1024 * 1024),
    )(place, subtree_end.reshape(BLOCKS, ROWS), queries, grad_out, saved_out, key_group, value_group)


def shards(queries, keys, values, saved_out, grad_out, normed_input, subtree_end):
    row_count = queries.shape[0]
    tensor_count = lax.axis_size("tensor")
    group_tokens = row_count * tensor_count
    key_group, value_group = (
        lax.all_gather(keys, "tensor", axis=0, tiled=True),
        lax.all_gather(values, "tensor", axis=0, tiled=True),
    )
    grad_queries, key_terms, value_terms = attention(
        queries, grad_out, saved_out, key_group, value_group, subtree_end
    )
    key_local, value_local = (
        lax.psum_scatter(key_terms, "tensor", scatter_dimension=0, tiled=True),
        lax.psum_scatter(value_terms, "tensor", scatter_dimension=0, tiled=True),
    )
    grad_keys = key_local.astype(jnp.bfloat16)
    grad_values = value_local.astype(jnp.bfloat16)
    key_group_grad = lax.all_gather(grad_keys, "tensor", axis=0, tiled=True)
    value_group_grad = lax.all_gather(grad_values, "tensor", axis=0, tiled=True)
    group_count = lax.axis_size("dp")
    feature_width = D // (group_count * tensor_count)
    split_input = normed_input.reshape(row_count, group_count, tensor_count, feature_width)
    columns = lax.all_to_all(split_input, "tensor", split_axis=2, concat_axis=0, tiled=True)
    columns = columns.reshape(group_tokens, group_count * feature_width)
    contract = (((0,), (0,)), ((), ()))
    key_weight = lax.dot_general(columns, key_group_grad, contract, preferred_element_type=f32)
    value_weight = lax.dot_general(columns, value_group_grad, contract, preferred_element_type=f32)
    key_weight = key_weight.reshape(group_count, feature_width, KVH * HD)
    value_weight = value_weight.reshape(group_count, feature_width, KVH * HD)
    summed_keys, summed_values = (
        lax.psum_scatter(key_weight, "dp", scatter_dimension=0, tiled=True),
        lax.psum_scatter(value_weight, "dp", scatter_dimension=0, tiled=True),
    )
    grad_wk = summed_keys.reshape(feature_width, KVH * HD)
    grad_wv = summed_values.reshape(feature_width, KVH * HD)
    return (grad_queries, grad_keys, grad_values, grad_wk, grad_wv)


def solution(mesh):
    rows = P(("dp", "tensor"), None)
    return jax.shard_map(
        shards, mesh=mesh, in_specs=(rows,) * 6 + (P("dp"),), out_specs=(rows,) * 5, check_vma=False
    )
```

time: 688 us -> 489 us (0.71)
  waiting for transfers between devices: 496 us -> 402 us
  local copies, waits for them, and re-layouts: 53.5 us -> 4.76 us
  matrix products: 52 us -> 7.62 us
  other arithmetic: 27 us -> 0 us
  Pallas kernels: 0 us -> 22.1 us
    reduce_scatter x1, waiting for transfers between devices: 219 us -> 66 us  [shards(): lax.psum_scatter(value_terms, 'tensor', scatter_dimension=0, tiled=True)]
    dot_general x6 -> x0, matrix products: 44.3 us -> none  [the longest x2 15.3 us: scores_for(): jnp.einsum('rgqd,bgd->gqrb', query_heads, key_heads, preferred_element_ty...]
    unnamed x14 -> x1, local copies, waits for them, and re-layouts: 31.1 us -> 3.22 us
    all_gather x1, waiting for transfers between devices: 13.7 us -> 37.9 us  [shards(): lax.all_gather(keys, 'tensor', axis=0, tiled=True)]
    pallas_call x0 -> x1, Pallas kernels: none -> 22.1 us  [attention(): pl.pallas_call(attention_kernel, grid_spec=pltpu.PrefetchScalarGridSpec(n...]
    all_gather x1, waiting for transfers between devices: 15.1 us -> 35.8 us  [shards(): lax.all_gather(values, 'tensor', axis=0, tiled=True)]
    reduce_scatter x1, waiting for transfers between devices: 64.8 us -> 75.7 us  [shards(): lax.psum_scatter(value_weight, 'dp', scatter_dimension=0, tiled=True)]
    reduce_sum x1 -> x0, other arithmetic: 9.71 us -> none  [total_active(): jnp.sum(jnp.where(allowed, jnp.exp(scores - raised[..., None]), 0.0), axi...]
  transfers between devices with their start and end apart: 8 -> 8, of which waited for: 8 -> 8; matrix products, arithmetic and copies ran while one was open for 11% -> 3% of each run, Pallas kernels for 0% -> 0%
where the time goes in v1:
time: 489 us; the launch traced here: 488 us
  waiting for transfers between devices  402 us (82%)
  blocking collectives  37.6 us (8%)
  Pallas kernels  22.1 us (5%)
  between operations  14.2 us (3%)
  matrix products  7.62 us (2%)
    reduce_scatter x1, waiting for transfers between devices, shards(): lax.psum_scatter(value_weight, 'dp', scatter_dimension=0, tiled=True)  75.7 us
    reduce_scatter x1, waiting for transfers between devices, shards(): lax.psum_scatter(key_terms, 'tensor', scatter_dimension=0, tiled=True)  74.2 us
    reduce_scatter x1, waiting for transfers between devices, shards(): lax.psum_scatter(key_weight, 'dp', scatter_dimension=0, tiled=True)  72.1 us
    reduce_scatter x1, waiting for transfers between devices, shards(): lax.psum_scatter(value_terms, 'tensor', scatter_dimension=0, tiled=True)  66 us
    all_gather x1, waiting for transfers between devices, shards(): lax.all_gather(keys, 'tensor', axis=0, tiled=True)  37.9 us
    all_to_all x1, blocking collectives, shards(): lax.all_to_all(split_input, 'tensor', split_axis=2, concat_axis=0, tiled=...  37.6 us
    all_gather x1, waiting for transfers between devices, shards(): lax.all_gather(values, 'tensor', axis=0, tiled=True)  35.8 us
    all_gather x1, waiting for transfers between devices, shards(): value_group_grad = lax.all_gather(grad_values, 'tensor', axis=0, tiled=True)  32.7 us
  transfers between devices with their start and end apart: 8, of which 8 were waited for; matrix products, arithmetic and copies ran while one was open for 3% of the time, Pallas kernels for 0%

profile of v1, /device:TPU:0, one launch (start us, length us, event | category | flops | bytes accessed | tf_op | source)
XLA Modules:
  0.0 488.4 jit_solution(12692823610820745164)
XLA Ops:
  7.2 0.0 all-gather.5.cloned.1.call-start
  7.2 0.7 all-gather.5.cloned.1.call-update
  7.9 0.0 all-gather.7.cloned.1.call-start
  7.9 0.7 all-gather.7.cloned.1.call-update
  8.6 0.0 reduce-scatter.5.cloned.1.call-start
  8.7 37.9 %all-gather.5.cloned.1.call-done.k_ref = bf16[2048,512]{1,0:T(8,128)(2,1)} async-done(((bf16[128,512]{1,0:T(8,128)(2,1)}), bf16[2048,512]{1,0:T(8,128)(2,1)}) %all-gather.5.cloned.1.call-update) | async-done | bytes 2097168 | tf_op jit(solution)/shard_map/all_gather | solution.py:178
  46.6 35.8 %all-gather.7.cloned.1.call-done.v_ref = bf16[2048,512]{1,0:T(8,128)(2,1)} async-done(((bf16[128,512]{1,0:T(8,128)(2,1)}), bf16[2048,512]{1,0:T(8,128)(2,1)}) %all-gather.7.cloned.1.call-update) | async-done | bytes 2097168 | tf_op jit(solution)/shard_map/all_gather | solution.py:179
  82.3 22.1 %shard_map.110 = (bf16[128,8192]{1,0:T(8,128)(2,1)}, bf16[2048,512]{1,0:T(8,128)(2,1)}, bf16[2048,512]{1,0:T(8,128)(2,1)}) custom-call(s32[1]{0:T(128)} %bitcast.place_ref, s32[16,128]{1,0:T(8,128)} %bitcast.31, bf16[128,8192]{1,0:T(8,128)(2,1)} %q_ref.1, bf16[128,8192]{1,0:T(8,128)(2,1)} %do_ref.1, bf16[128,8192]{1,0:T(8,128)(2,1)} %o_ref.1, ...), custom_call_target="tpu_custom_call" | custom-call | tf_op jit(solution)/shard_map/pallas_call | solution.py:146
  104.4 0.0 reduce-scatter.5.cloned.1.call-update
  104.4 0.0 reduce-scatter.7.cloned.1.call-start
  104.5 0.5 reduce-scatter.7.cloned.1.call-update
  105.0 0.0 all-gather.9.cloned.1.call-start
  105.1 74.2 %reduce-scatter.5.cloned.1.call-done = bf16[128,512]{1,0:T(8,128)(2,1)} async-done(((bf16[2048,512]{1,0:T(8,128)(2,1)}), bf16[128,512]{1,0:T(8,128)(2,1)}) %reduce-scatter.5.cloned.1.call-update) | async-done | bytes 131088 | tf_op jit(solution)/shard_map/reduce_scatter | solution.py:185
  179.3 0.0 all-gather.9.cloned.1.call-update
  179.3 0.0 all-gather.11.cloned.1.call-start
  179.4 66.0 %reduce-scatter.7.cloned.1.call-done = bf16[128,512]{1,0:T(8,128)(2,1)} async-done(((bf16[2048,512]{1,0:T(8,128)(2,1)}), bf16[128,512]{1,0:T(8,128)(2,1)}) %reduce-scatter.7.cloned.1.call-update) | async-done | bytes 131088 | tf_op jit(solution)/shard_map/reduce_scatter | solution.py:186
  245.4 0.0 all-gather.11.cloned.1.call-update
  245.4 0.0 reduce-scatter.9.cloned.1.call-start
  245.5 3.2 copy.14
  248.7 0.2 copy.15
  248.9 37.6 %all_to_all.15 = bf16[128,8,16,64]{0,3,1,2:T(8,128)(2,1)S(1)} all-to-all(bf16[128,8,16,64]{0,3,1,2:T(8,128)(2,1)S(1)} %copy.15), channel_id=1, replica_groups=mesh['dp'=8,'tensor'=16] {'tensor'}, dimensions={2} | all-to-all | bytes 4194304 | tf_op jit(solution)/shard_map/all_to_all | solution.py:195
  286.5 1.4 copy.16
  287.8 5.5 %all-gather.9.cloned.1.call-done = bf16[2048,512]{1,0:T(8,128)(2,1)} async-done(((bf16[128,512]{1,0:T(8,128)(2,1)}), bf16[2048,512]{1,0:T(8,128)(2,1)}) %all-gather.9.cloned.1.call-update) | async-done | bytes 2097168 | tf_op jit(solution)/shard_map/all_gather | solution.py:190
  293.3 3.8 fusion
  297.2 0.0 reduce-scatter.9.cloned.1.call-update
  297.2 0.0 reduce-scatter.11.cloned.1.call-start
  297.2 32.7 %all-gather.11.cloned.1.call-done = bf16[2048,512]{1,0:T(8,128)(2,1)} async-done(((bf16[128,512]{1,0:T(8,128)(2,1)}), bf16[2048,512]{1,0:T(8,128)(2,1)}) %all-gather.11.cloned.1.call-update) | async-done | bytes 2097168 | tf_op jit(solution)/shard_map/all_gather | solution.py:191
  329.9 3.8 fusion.2
  333.7 0.0 reduce-scatter.11.cloned.1.call-update
  333.7 72.1 %reduce-scatter.9.cloned.1.call-done = f32[1,64,512]{2,1,0:T(8,128)} async-done(((f32[8,64,512]{2,1,0:T(8,128)}), f32[1,64,512]{2,1,0:T(8,128)}) %reduce-scatter.9.cloned.1.call-update) | async-done | bytes 131088 | tf_op jit(solution)/shard_map/reduce_scatter | solution.py:203
  405.9 75.7 %reduce-scatter.11.cloned.1.call-done = f32[1,64,512]{2,1,0:T(8,128)} async-done(((f32[8,64,512]{2,1,0:T(8,128)}), f32[1,64,512]{2,1,0:T(8,128)}) %reduce-scatter.11.cloned.1.call-update) | async-done | bytes 131088 | tf_op jit(solution)/shard_map/reduce_scatter | solution.py:204
Async XLA Ops:
  7.2 39.4 %all-gather.5.cloned.1.call-start = ((), (), s32[]{:S(2)}) async-start(), calls=%async_computation.5 | async-start | bytes 2228224 | tf_op jit(solution)/shard_map/all_gather | solution.py:178
  7.9 74.4 %all-gather.7.cloned.1.call-start = ((), (), s32[]{:S(2)}) async-start(), calls=%async_computation.6 | async-start | bytes 2228224 | tf_op jit(solution)/shard_map/all_gather | solution.py:179
  8.6 170.7 %reduce-scatter.5.cloned.1.call-start = ((), (), s32[]{:S(2)}) async-start(), calls=%async_computation.7 | async-start | bytes 2228224 | tf_op jit(solution)/shard_map/reduce_scatter | solution.py:185
  104.4 141.0 %reduce-scatter.7.cloned.1.call-start = ((), (), s32[]{:S(2)}) async-start(), calls=%async_computation.8 | async-start | bytes 2228224 | tf_op jit(solution)/shard_map/reduce_scatter | solution.py:186
  105.0 188.3 %all-gather.9.cloned.1.call-start = ((), (), s32[]{:S(2)}) async-start(), calls=%async_computation.9 | async-start | bytes 2228224 | tf_op jit(solution)/shard_map/all_gather | solution.py:190
  179.3 150.6 %all-gather.11.cloned.1.call-start = ((), (), s32[]{:S(2)}) async-start(), calls=%async_computation.11 | async-start | bytes 2228224 | tf_op jit(solution)/shard_map/all_gather | solution.py:191
  245.4 160.4 %reduce-scatter.9.cloned.1.call-start = ((), (), s32[]{:S(2)}) async-start(), calls=%async_computation.10 | async-start | bytes 1179648 | tf_op jit(solution)/shard_map/reduce_scatter | solution.py:203
  297.2 184.4 %reduce-scatter.11.cloned.1.call-start = ((), (), s32[]{:S(2)}) async-start(), calls=%async_computation.12 | async-start | bytes 1179648 | tf_op jit(solution)/shard_map/reduce_scatter | solution.py:204
Sparse Core Ops, SparseCore 0:
  9.7 36.8 all-gather.4
  48.3 34.0 all-gather.6
  104.6 74.7 reduce-scatter.4
  182.1 63.2 reduce-scatter.6
  247.5 45.7 all-gather.8
  295.5 34.3 all-gather.10
  334.1 71.7 reduce-scatter.8
  410.5 70.9 reduce-scatter.10

commit v2 on v1

--- a/solution.py
+++ b/solution.py
@@ -1,5 +1,4 @@
 import functools
-import math
 
 import jax
 import jax.numpy as jnp
@@ -27,7 +26,7 @@
 
 def attention_kernel(
     place_ref, end_ref, q_ref, do_ref, o_ref, k_ref, v_ref,
-    dq_ref, dk_ref, dv_ref, rank, pick, bias, kc, vc,
+    dq_ref, dkv_ref, rank, pick, bias, kc, vc,
 ):
     t = place_ref[0]
     g = pl.program_id(0)
@@ -126,10 +125,10 @@
         dk = (dk_acc * SCALE).astype(bf16)
         dv = dv_acc.astype(bf16)
         chosen = pick[0:width, :]
-        dk_ref[...] = lax.dot_general(chosen, dk[ROWS:], TN, preferred_element_type=f32).astype(bf16)
-        dv_ref[...] = lax.dot_general(chosen, dv[ROWS:], TN, preferred_element_type=f32).astype(bf16)
-        dk_ref[pl.ds(pl.multiple_of(first, ROWS), ROWS), :] = dk[:ROWS]
-        dv_ref[pl.ds(pl.multiple_of(first, ROWS), ROWS), :] = dv[:ROWS]
+        dkv_ref[0] = lax.dot_general(chosen, dk[ROWS:], TN, preferred_element_type=f32).astype(bf16)
+        dkv_ref[1] = lax.dot_general(chosen, dv[ROWS:], TN, preferred_element_type=f32).astype(bf16)
+        dkv_ref[0, pl.ds(pl.multiple_of(first, ROWS), ROWS), :] = dk[:ROWS]
+        dkv_ref[1, pl.ds(pl.multiple_of(first, ROWS), ROWS), :] = dv[:ROWS]
 
     lower = -1
     for width in WIDTHS:
@@ -141,7 +140,7 @@
     place = lax.axis_index("tensor").astype(jnp.int32).reshape(1)
     wide = pl.BlockSpec((ROWS, HG * HD), lambda g, place: (0, g))
     whole = pl.BlockSpec((SEQ, KVH * HD), lambda g, place: (0, 0))
-    part = pl.BlockSpec((SEQ, HD), lambda g, place: (0, g))
+    part = pl.BlockSpec((2, SEQ, HD), lambda g, place: (0, 0, g))
     far_most = SEQ - ROWS
     return pl.pallas_call(
         attention_kernel,
@@ -152,7 +151,7 @@
                 pl.BlockSpec((BLOCKS, ROWS), lambda g, place: (0, 0)),
                 wide, wide, wide, whole, whole,
             ],
-            out_specs=[wide, part, part],
+            out_specs=[wide, part],
             scratch_shapes=[
                 pltpu.VMEM((BLOCKS, ROWS), jnp.int32),
                 pltpu.VMEM((far_most, SEQ), bf16),
@@ -163,49 +162,393 @@
         ),
         out_shape=[
             jax.ShapeDtypeStruct((ROWS, HQ * HD), bf16),
-            jax.ShapeDtypeStruct((SEQ, KVH * HD), bf16),
-            jax.ShapeDtypeStruct((SEQ, KVH * HD), bf16),
+            jax.ShapeDtypeStruct((2, SEQ, KVH * HD), bf16),
         ],
         compiler_params=pltpu.CompilerParams(vmem_limit_bytes=56 * 1024 * 1024),
     )(place, subtree_end.reshape(BLOCKS, ROWS), queries, grad_out, saved_out, key_group, value_group)
 
 
+MESH = pl.DeviceIdType.MESH
+KV = KVH * HD
+HALF = KV // 2
+FEAT = 2048
+ORDER = (1, 3, 2)
+
+
+def coords():
+    d, t = lax.axis_index("dp"), lax.axis_index("tensor")
+    return d // 4, d % 4, t // 4, (t // 2) % 2, t % 2
+
+
+def device(yh, x, z, yl, c):
+    return (yh * 4 + x, z * 4 + yl * 2 + c)
+
+
+def greet(peers):
+    barrier = pltpu.get_barrier_semaphore()
+    for peer in peers:
+        pl.semaphore_signal(barrier, inc=1, device_id=peer, device_id_type=MESH)
+    pl.semaphore_wait(barrier, len(peers))
+
+
+class Sender:
+    def __init__(self, send_sem, recv_sem):
+        self.sems, self.all = (send_sem, recv_sem), []
+
+    def __call__(self, src, dst, peer):
+        i = len(self.all)
+        copy = pltpu.make_async_remote_copy(
+            src_ref=src, dst_ref=dst, send_sem=self.sems[0].at[i], recv_sem=self.sems[1].at[i],
+            device_id=peer, device_id_type=MESH,
+        )
+        copy.start()
+        self.all.append(copy)
+        return copy
+
+    def finish(self):
+        for copy in self.all:
+            copy.wait_send()
+
+
+GATHER_COPIES = 30 + 9
+
+
+def gather_kernel(k_ref, v_ref, n_ref, k_all, v_all, cols, send_sem, recv_sem, local_sem):
+    yh, x, z, yl, c = coords()
+    y_peer = device(yh, x, z, 1 - yl, c)
+    core_peer = device(yh, x, z, yl, 1 - c)
+    z_peer = {d: device(yh, x, (z + d) % 4, yl, c) for d in (1, 2, 3)}
+    x_peer = {d: device(yh, (x + d) % 4, z, yl, c) for d in (1, 3)}
+    greet([y_peer, core_peer, *z_peer.values(), *x_peer.values()])
+    send = Sender(send_sem, recv_sem)
+
+    def rows(zz, yy):
+        return pl.ds(pl.multiple_of((zz * 4 + yy * 2 + c) * ROWS, ROWS), ROWS)
+
+    def columns(part, xx):
+        return pl.ds(pl.multiple_of(part * (D // 2) + xx * 1024, 1024), 1024)
+
+    mine = rows(z, yl)
+    first = send(k_ref, k_all.at[mine], y_peer)
+    k_z = {d: send(k_ref, k_all.at[mine], z_peer[d]) for d in ORDER}
+    v_z = {d: send(v_ref, v_all.at[mine], z_peer[d]) for d in ORDER}
+    v_y = send(v_ref, v_all.at[mine], y_peer)
+    slot_of = {0: 0, 1: 1, 3: 2}
+    n_x = {}
+    for d in (1, 3):
+        for part in (0, 1):
+            n_x[d, part] = send(
+                n_ref.at[:, columns(part, (x + d) % 4)],
+                cols.at[slot_of[4 - d], c, :, pl.ds(part * 1024, 1024)],
+                x_peer[d],
+            )
+    local = [
+        pltpu.make_async_copy(k_ref, k_all.at[mine], local_sem.at[0]),
+        pltpu.make_async_copy(v_ref, v_all.at[mine], local_sem.at[1]),
+    ]
+    for part in (0, 1):
+        local.append(
+            pltpu.make_async_copy(
+                n_ref.at[:, columns(part, x)],
+                cols.at[0, c, :, pl.ds(part * 1024, 1024)],
+                local_sem.at[2 + part],
+            )
+        )
+    for copy in local:
+        copy.start()
+    crossed = [send(k_ref, k_all.at[mine], core_peer), send(v_ref, v_all.at[mine], core_peer)]
+    for part in (0, 1):
+        crossed.append(
+            send(
+                n_ref.at[:, columns(part, x)],
+                cols.at[0, c, :, pl.ds(part * 1024, 1024)],
+                core_peer,
+            )
+        )
+
+    def cross(whole, zz, yy):
+        crossed.append(send(whole.at[rows(zz, yy)], whole.at[rows(zz, yy)], core_peer))
+
+    first.wait_recv()
+    other = rows(z, 1 - yl)
+    k_yz = {d: send(k_all.at[other], k_all.at[other], z_peer[d]) for d in ORDER}
+    cross(k_all, z, 1 - yl)
+    v_zy = {}
+    for d in ORDER:
+        from_z = (z + 4 - d) % 4
+        v_z[d].wait_recv()
+        v_zy[d] = send(v_all.at[rows(from_z, yl)], v_all.at[rows(from_z, yl)], y_peer)
+        cross(v_all, from_z, yl)
+    for d in ORDER:
+        k_z[d].wait_recv()
+        cross(k_all, (z + 4 - d) % 4, yl)
+    v_y.wait_recv()
+    cross(v_all, z, 1 - yl)
+    for d in (1, 3):
+        for part in (0, 1):
+            n_x[d, part].wait_recv()
+        place = cols.at[slot_of[4 - d], c]
+        crossed.append(send(place, place, core_peer))
+    for d in ORDER:
+        k_yz[d].wait_recv()
+        cross(k_all, (z + 4 - d) % 4, 1 - yl)
+    for d in ORDER:
+        v_zy[d].wait_recv()
+        cross(v_all, (z + 4 - d) % 4, 1 - yl)
+    for copy in crossed:
+        copy.wait_recv()
+    for copy in local:
+        copy.wait()
+    send.finish()
+
+
+def gather(keys, values, normed_input):
+    return pl.pallas_call(
+        gather_kernel,
+        in_specs=[pl.BlockSpec(memory_space=pl.ANY)] * 3,
+        out_specs=[pl.BlockSpec(memory_space=pl.ANY)] * 3,
+        out_shape=[
+            jax.ShapeDtypeStruct((SEQ, KV), bf16),
+            jax.ShapeDtypeStruct((SEQ, KV), bf16),
+            jax.ShapeDtypeStruct((3, 2, ROWS, FEAT), bf16),
+        ],
+        scratch_shapes=[
+            pltpu.SemaphoreType.DMA((GATHER_COPIES,)),
+            pltpu.SemaphoreType.DMA((GATHER_COPIES,)),
+            pltpu.SemaphoreType.DMA((4,)),
+        ],
+        compiler_params=pltpu.CompilerParams(collective_id=0, has_side_effects=True),
+    )(keys, values, normed_input)
+
+
+SUM_COPIES = 56
+
+
+def sum_kernel(
+    part_ref, n_ref, cols_ref, gk_ref, gv_ref, wk_ref, wv_ref,
+    cols, own, came, a1, b1, a1_in, b1_in, b2, b2_in, a2, a2_in, grads, g_in,
+    wa, wb, wa_in, wb_in, wa2, wb2, wa2_in, wb2_in, w_own, w_in,
+    send_sem, recv_sem, local_sem,
+):
+    yh, x, z, yl, c = coords()
+    y = yh * 2 + yl
+    y_peer = device(yh, x, z, 1 - yl, c)
+    core_peer = device(yh, x, z, yl, 1 - c)
+    z_at = {d: (z + d) % 4 for d in range(4)}
+    y_at = {d: (y + d) % 4 for d in range(4)}
+    z_peer = {d: device(yh, x, z_at[d], yl, c) for d in ORDER}
+    y_ring = {d: device(y_at[d] // 2, x, z, y_at[d] % 2, c) for d in ORDER}
+    x_peer = {d: device(yh, (x + d) % 4, z, yl, c) for d in ORDER}
+    greet([core_peer, *z_peer.values(), *y_ring.values(), *x_peer.values()])
+    send = Sender(send_sem, recv_sem)
+
+    local, cross = {}, {}
+    for i, d in enumerate((1, 3, 2, 0)):
+        cross[d] = send(part_ref.at[1 - c, z_at[d]], came.at[z_at[d]], core_peer)
+        local[d] = pltpu.make_async_copy(part_ref.at[c, z_at[d]], own.at[z_at[d]], local_sem.at[i])
+        local[d].start()
+    n_x = []
+    for part in (0, 1):
+        start = pl.multiple_of(part * (D // 2) + ((x + 2) % 4) * 1024, 1024)
+        n_x.append(
+            send(
+                n_ref.at[:, pl.ds(start, 1024)],
+                cols.at[2, c, :, pl.ds(part * 1024, 1024)],
+                x_peer[2],
+            )
+        )
+    loads = []
+    for slot, d in ((0, 0), (1, 1), (2, 3)):
+        copy = pltpu.make_async_copy(cols_ref.at[slot], cols.at[d], local_sem.at[4 + slot])
+        copy.start()
+        loads.append(copy)
+
+    a_z, b_y = {}, {}
+    for d in (1, 3, 2, 0):
+        at = z_at[d]
+        cross[d].wait_recv()
+        local[d].wait()
+        for yy in (0, 1):
+            total = own[at, yy].astype(f32) + came[at, yy].astype(f32)
+            a1[at, yy] = total[:, :HALF].astype(bf16)
+            b1[at, yy] = total[:, HALF:].astype(bf16)
+        if d:
+            a_z[d] = send(a1.at[at], a1_in.at[d - 1], z_peer[d])
+        b_y[d] = send(b1.at[at, 1 - yl], b1_in.at[at], y_peer)
+    b_z = {}
+    for d in ORDER:
+        at = z_at[d]
+        b_y[d].wait_recv()
+        b2[d - 1] = (b1[at, yl].astype(f32) + b1_in[at].astype(f32)).astype(bf16)
+        b_z[d] = send(b2.at[d - 1], b2_in.at[d - 1], z_peer[d])
+    for d in ORDER:
+        a_z[d].wait_recv()
+
+    def left(yy):
+        total = a1[z, yy].astype(f32)
+        for d in ORDER:
+            total = total + a1_in[d - 1, yy].astype(f32)
+        return total
+
+    a2[...] = left(1 - yl).astype(bf16)
+    a_y = send(a2, a2_in, y_peer)
+    kept = left(yl)
+    a_y.wait_recv()
+    grads[0, :, :HALF] = (kept + a2_in[...].astype(f32)).astype(bf16)
+    g_x = []
+    for d in ORDER:
+        g_x.append(
+            send(
+                grads.at[0, :, pl.ds(0, HALF)], grads.at[4 - d, :, pl.ds(0, HALF)], x_peer[d]
+            )
+        )
+    b_y[0].wait_recv()
+    total = b1[z, yl].astype(f32) + b1_in[z].astype(f32)
+    for d in ORDER:
+        b_z[d].wait_recv()
+        total = total + b2_in[d - 1].astype(f32)
+    grads[0, :, HALF:] = total.astype(bf16)
+    for d in ORDER:
+        g_x.append(
+            send(
+                grads.at[0, :, pl.ds(HALF, HALF)], grads.at[4 - d, :, pl.ds(HALF, HALF)], x_peer[d]
+            )
+        )
+    theirs = pl.ds(pl.multiple_of((1 - c) * ROWS, ROWS), ROWS)
+    ours = pl.ds(pl.multiple_of(c * ROWS, ROWS), ROWS)
+    g_core = send(grads.at[0, theirs], g_in, core_peer)
+    for copy in n_x:
+        copy.wait_recv()
+    n_core = send(cols.at[2, c], cols.at[2, c], core_peer)
+    g_core.wait_recv()
+    is_key = c == 0
+    mine, other = grads[0, ours, :].astype(f32), g_in[...].astype(f32)
+    gk_ref[...] = jnp.where(is_key, mine, other).astype(bf16)
+    gv_ref[...] = jnp.where(is_key, other, mine).astype(bf16)
+    for copy in loads:
+        copy.wait()
+    n_core.wait_recv()
+    for copy in g_x:
+        copy.wait_recv()
+
+    right_side = grads[...].reshape(4 * 2 * ROWS, KV)
+    w_a, w_b = {}, {}
+    for d in (1, 3, 2, 0):
+        at = z_at[d]
+        for top in (0, 1):
+            start = pl.multiple_of(top * 1024 + at * 256, 256)
+            left_side = cols[:, :, :, pl.ds(start, 256)].reshape(4 * 2 * ROWS, 256)
+            block = lax.dot_general(left_side, right_side, TN, preferred_element_type=f32)
+            block = block.astype(bf16)
+            for low in (0, 1):
+                piece = block[low * ROWS : (low + 1) * ROWS]
+                wa[at, top * 2 + low] = piece[:, :HALF]
+                wb[top * 2 + low, at] = piece[:, HALF:]
+        if d:
+            w_a[d] = send(wa.at[at], wa_in.at[d - 1], z_peer[d])
+    for d in ORDER:
+        w_b[d] = send(wb.at[y_at[d]], wb_in.at[d - 1], y_ring[d])
+    for d in ORDER:
+        w_a[d].wait_recv()
+
+    def over_z(yy):
+        total = wa[z, yy].astype(f32)
+        for d in ORDER:
+            total = total + wa_in[d - 1, yy].astype(f32)
+        return total
+
+    w_ay, w_bz = {}, {}
+    for d in ORDER:
+        wa2[d - 1] = over_z(y_at[d]).astype(bf16)
+        w_ay[d] = send(wa2.at[d - 1], wa2_in.at[d - 1], y_ring[d])
+    for d in ORDER:
+        w_b[d].wait_recv()
+
+    def over_y(zz):
+        total = wb[y, zz].astype(f32)
+        for d in ORDER:
+            total = total + wb_in[d - 1, zz].astype(f32)
+        return total
+
+    for d in ORDER:
+        wb2[d - 1] = over_y(z_at[d]).astype(bf16)
+        w_bz[d] = send(wb2.at[d - 1], wb2_in.at[d - 1], z_peer[d])
+    total = over_z(y)
+    for d in ORDER:
+        w_ay[d].wait_recv()
+        total = total + wa2_in[d - 1].astype(f32)
+    w_own[:, :HALF] = total
+    total = over_y(z)
+    for d in ORDER:
+        w_bz[d].wait_recv()
+        total = total + wb2_in[d - 1].astype(f32)
+    w_own[:, HALF:] = total
+    theirs = pl.ds(pl.multiple_of((1 - c) * 64, 64), 64)
+    ours = pl.ds(pl.multiple_of(c * 64, 64), 64)
+    w_core = send(w_own.at[theirs], w_in, core_peer)
+    mine = w_own[ours, :]
+    w_core.wait_recv()
+    other = w_in[...]
+    wk_ref[...] = jnp.where(is_key, mine, other)
+    wv_ref[...] = jnp.where(is_key, other, mine)
+    send.finish()
+
+
+def sums(parts, normed_input, cols):
+    vmem = lambda *shape: pltpu.VMEM(shape, bf16)
+    anywhere = pl.BlockSpec(memory_space=pl.ANY)
+    inside = pl.BlockSpec(memory_space=pltpu.VMEM)
+    R2 = 2 * ROWS
+    return pl.pallas_call(
+        sum_kernel,
+        in_specs=[anywhere] * 3,
+        out_specs=[inside] * 4,
+        out_shape=[
+            jax.ShapeDtypeStruct((ROWS, KV), bf16),
+            jax.ShapeDtypeStruct((ROWS, KV), bf16),
+            jax.ShapeDtypeStruct((64, KV), f32),
+            jax.ShapeDtypeStruct((64, KV), f32),
+        ],
+        scratch_shapes=[
+            vmem(4, 2, ROWS, FEAT),
+            vmem(4, 2, R2, KV),
+            vmem(4, 2, R2, KV),
+            vmem(4, 2, R2, HALF),
+            vmem(4, 2, R2, HALF),
+            vmem(3, 2, R2, HALF),
+            vmem(4, R2, HALF),
+            vmem(3, R2, HALF),
+            vmem(3, R2, HALF),
+            vmem(R2, HALF),
+            vmem(R2, HALF),
+            vmem(4, R2, KV),
+            vmem(ROWS, KV),
+            vmem(4, 4, ROWS, HALF),
+            vmem(4, 4, ROWS, HALF),
+            vmem(3, 4, ROWS, HALF),
+            vmem(3, 4, ROWS, HALF),
+            vmem(3, ROWS, HALF),
+            vmem(3, ROWS, HALF),
+            vmem(3, ROWS, HALF),
+            vmem(3, ROWS, HALF),
+            pltpu.VMEM((ROWS, KV), f32),
+            pltpu.VMEM((64, KV), f32),
+            pltpu.SemaphoreType.DMA((SUM_COPIES,)),
+            pltpu.SemaphoreType.DMA((SUM_COPIES,)),
+            pltpu.SemaphoreType.DMA((7,)),
+        ],
+        compiler_params=pltpu.CompilerParams(
+            collective_id=1, has_side_effects=True, vmem_limit_bytes=48 * 1024 * 1024
+        ),
+    )(parts.reshape(2, 4, 2, R2, KV), normed_input, cols)
+
+
 def shards(queries, keys, values, saved_out, grad_out, normed_input, subtree_end):
-    row_count = queries.shape[0]
-    tensor_count = lax.axis_size("tensor")
-    group_tokens = row_count * tensor_count
-    key_group, value_group = (
-        lax.all_gather(keys, "tensor", axis=0, tiled=True),
-        lax.all_gather(values, "tensor", axis=0, tiled=True),
-    )
-    grad_queries, key_terms, value_terms = attention(
+    key_group, value_group, cols = gather(keys, values, normed_input)
+    grad_queries, parts = attention(
         queries, grad_out, saved_out, key_group, value_group, subtree_end
     )
-    key_local, value_local = (
-        lax.psum_scatter(key_terms, "tensor", scatter_dimension=0, tiled=True),
-        lax.psum_scatter(value_terms, "tensor", scatter_dimension=0, tiled=True),
-    )
-    grad_keys = key_local.astype(jnp.bfloat16)
-    grad_values = value_local.astype(jnp.bfloat16)
-    key_group_grad = lax.all_gather(grad_keys, "tensor", axis=0, tiled=True)
-    value_group_grad = lax.all_gather(grad_values, "tensor", axis=0, tiled=True)
-    group_count = lax.axis_size("dp")
-    feature_width = D // (group_count * tensor_count)
-    split_input = normed_input.reshape(row_count, group_count, tensor_count, feature_width)
-    columns = lax.all_to_all(split_input, "tensor", split_axis=2, concat_axis=0, tiled=True)
-    columns = columns.reshape(group_tokens, group_count * feature_width)
-    contract = (((0,), (0,)), ((), ()))
-    key_weight = lax.dot_general(columns, key_group_grad, contract, preferred_element_type=f32)
-    value_weight = lax.dot_general(columns, value_group_grad, contract, preferred_element_type=f32)
-    key_weight = key_weight.reshape(group_count, feature_width, KVH * HD)
-    value_weight = value_weight.reshape(group_count, feature_width, KVH * HD)
-    summed_keys, summed_values = (
-        lax.psum_scatter(key_weight, "dp", scatter_dimension=0, tiled=True),
-        lax.psum_scatter(value_weight, "dp", scatter_dimension=0, tiled=True),
-    )
-    grad_wk = summed_keys.reshape(feature_width, KVH * HD)
-    grad_wv = summed_values.reshape(feature_width, KVH * HD)
-    return (grad_queries, grad_keys, grad_values, grad_wk, grad_wv)
+    return (grad_queries, *sums(parts, normed_input, cols))
 
 
 def solution(mesh):

time: 489 us -> 131 us (0.27)
  waiting for transfers between devices: 402 us -> 0 us
  Pallas kernels: 22.1 us -> 127 us
  blocking collectives: 37.6 us -> 0 us
  between operations: 14.2 us -> 0.67 us
  matrix products: 7.62 us -> 0 us
    reduce_scatter x4 -> x0, waiting for transfers between devices: 288 us -> none  [the longest x1 75.7 us: shards(): lax.psum_scatter(value_weight, 'dp', scatter_dimension=0, tiled=True)]
    all_gather x4 -> x0, waiting for transfers between devices: 112 us -> none  [the longest x1 37.9 us: shards(): lax.all_gather(keys, 'tensor', axis=0, tiled=True)]
    pallas_call x0 -> x2, Pallas kernels: none -> 104 us  [the longest x1 74.5 us: sums(): pl.pallas_call(sum_kernel, in_specs=[anywhere] * 3, out_specs=[inside] *...]
    all_to_all x1 -> x0, blocking collectives: 37.6 us -> none  [shards(): lax.all_to_all(split_input, 'tensor', split_axis=2, concat_axis=0, tiled=...]
    dot_general x2 -> x0, matrix products: 7.62 us -> none  [the longest x1 3.82 us: shards(): lax.dot_general(columns, value_group_grad, contract, preferred_element_ty...]
  transfers between devices with their start and end apart: 8 -> 0, of which waited for: 8 -> 0; matrix products, arithmetic and copies ran while one was open for 3% -> 0% of each run, Pallas kernels for 0% -> 0%
where the time goes in v2:
time: 131 us; the launch traced here: 130 us
  Pallas kernels  127 us (97%)
  local copies, waits for them, and re-layouts  2.63 us (2%)
    pallas_call x1, Pallas kernels, sums(): pl.pallas_call(sum_kernel, in_specs=[anywhere] * 3, out_specs=[inside] *...  74.5 us
    pallas_call x1, Pallas kernels, gather(): pl.pallas_call(gather_kernel, in_specs=[pl.BlockSpec(memory_space=pl.ANY)...  30 us
    pallas_call x1, Pallas kernels, attention(): pl.pallas_call(attention_kernel, grid_spec=pltpu.PrefetchScalarGridSpec(n...  22.2 us
    unnamed x8, local copies, waits for them, and re-layouts  2.63 us

profile of v2, /device:TPU:0, one launch (start us, length us, event | category | flops | bytes accessed | tf_op | source)
XLA Modules:
  0.0 130.0 jit_solution(2684844347804014664)
XLA Ops:
  0.6 30.0 %shard_map.110 = (bf16[2048,512]{1,0:T(8,128)(2,1)}, bf16[2048,512]{1,0:T(8,128)(2,1)}, bf16[3,2,128,2048]{3,2,1,0:T(8,128)(2,1)}) custom-call(bf16[128,512]{1,0:T(8,128)(2,1)} %k_ref.1, bf16[128,512]{1,0:T(8,128)(2,1)} %v_ref.1, bf16[128,8192]{1,0:T(8,128)(2,1)} %n_ref.3), custom_call_target="tpu_custom_call" | custom-call | tf_op jit(solution)/shard_map/pallas_call | solution.py:306
  30.6 0.0 copy-start
  30.6 0.0 copy-start.1
  30.6 22.2 %shard_map.111 = (bf16[128,8192]{1,0:T(8,128)(2,1)}, bf16[2,2048,512]{2,1,0:T(8,128)(2,1)}) custom-call(s32[1]{0:T(128)} %bitcast.place_ref, s32[16,128]{1,0:T(8,128)} %bitcast.4, bf16[128,8192]{1,0:T(8,128)(2,1)} %q_ref.1, bf16[128,8192]{1,0:T(8,128)(2,1)} %do_ref.1, bf16[128,8192]{1,0:T(8,128)(2,1)} %o_ref.1, bf16[2048,512]{1,0:T(8,128)(2,1)} %get-tuple-element.14.k_ref, ...), custom_call_target="tpu_custom_call" | custom-call | tf_op jit(solution)/shard_map/pallas_call | solution.py:145
  52.8 0.0 copy-done
  52.8 0.0 copy-done.1
  52.9 74.5 %shard_map.112 = (bf16[128,512]{1,0:T(8,128)(2,1)S(1)}, bf16[128,512]{1,0:T(8,128)(2,1)S(1)}, f32[64,512]{1,0:T(8,128)S(1)}, f32[64,512]{1,0:T(8,128)S(1)}) custom-call(bf16[2,4,2,256,512]{4,3,2,1,0:T(8,128)(2,1)} %bitcast.3, bf16[128,8192]{1,0:T(8,128)(2,1)S(1)} %copy-done, bf16[3,2,128,2048]{3,2,1,0:T(8,128)(2,1)S(1)} %copy-done.1), custom_call_target="tpu_custom_call" | custom-call | tf_op jit(solution)/shard_map/pallas_call | solution.py:502
  127.4 0.7 copy.16
  128.0 0.7 copy.17
  128.7 0.7 copy.18
  129.3 0.7 copy.19
Async XLA Ops:
  30.6 22.2 %copy-start = (bf16[128,8192]{1,0:T(8,128)(2,1)S(1)}, bf16[128,8192]{1,0:T(8,128)(2,1)}, u32[]{:S(2)}) copy-start(bf16[128,8192]{1,0:T(8,128)(2,1)} %n_ref.3) | copy-start | bytes 6291460
  30.6 22.2 %copy-start.1 = (bf16[3,2,128,2048]{3,2,1,0:T(8,128)(2,1)S(1)}, bf16[3,2,128,2048]{3,2,1,0:T(8,128)(2,1)}, u32[]{:S(2)}) copy-start(bf16[3,2,128,2048]{3,2,1,0:T(8,128)(2,1)} %get-tuple-element.18.cols_ref) | copy-start | bytes 9437188
